TPU v7x, 32 devices: a whole 2x2x4 slice. The times are simulated.
32 devices in a mesh: grp: 2 (over y), mp: 16 (over z, x, core).
Axes of the slice: x: 2, y: 2, z: 4, core: 2. Of those that a mesh axis runs over, the one named last changes fastest.
Arguments:
- query_grad: bfloat16 [64, 8192], P('grp'), parts along dimension 0, may hold values from -0.0625 to 0.0625
- query_input: bfloat16 [64, 8192], P('grp'), parts along dimension 0, may hold values from -6 to 6
- query_ids: int32 [64], P('grp'), parts along dimension 0, may hold values from 0 to 7, never falling along the last dimension, each value on 1 to 8 neighbouring positions
- train_grad: bfloat16 [256, 8192], P('grp'), parts along dimension 0, may hold values from -0.0625 to 0.0625
- train_input: bfloat16 [256, 8192], P('grp'), parts along dimension 0, may hold values from -3 to 3
- train_ids: int32 [256], P('grp'), parts along dimension 0, may hold values from 0 to 15, never falling along the last dimension, each value on 1 to 16 neighbouring positions
- output_basis: bfloat16 [8192, 8192], P(None, 'mp'), may hold values from -0.0625 to 0.0625
- input_basis: bfloat16 [8192, 8192], P(None, 'mp'), may hold values from -0.0625 to 0.0625
- eigenvalues: float32 [8192, 8192], P('mp'), may hold values from 0.05 to 5
Outputs:
- scores: float32 [16, 16], P('grp'), parts along dimension 0
There are 2 independent parts, one for each index of `grp`. A program takes and returns all parts, laid end to end along the dimension named above; an argument that names none is the same for every part. Nothing has to cross between parts.
Inputs may be any that keep to these rules, and one draw needn't show every extreme that they name: `query_ids`: each query is a run of consecutive tokens, 1 to 8 long, one of exactly 8; ids never fall. `train_ids`: each training example is a run of consecutive tokens, 1 to 16 long, one of exactly 16; ids never fall.
All inputs are finite; a program needn't handle non-finite values.
Results may differ from a plain program's by a relative error of at most 0.0049.
Values may be sent and summed in bfloat16 or wider, within the bound.
A program may use at most 256 MiB of HBM per device.

v0:
```python
import math
import jax
import jax.numpy as jnp
from jax import lax
from jax.sharding import PartitionSpec as P

QUERIES = 8
QMOST = 8
TRAIN = 16
damping_shift = 0.25


def rotate(basis, factors):
    return lax.dot_general(
        basis, factors, (((0,), (1,)), ((), ())), preferred_element_type=jnp.float32
    ).astype(jnp.bfloat16)


def query_window(query_ids):
    token_count = query_ids.shape[0]
    labels = jnp.arange(QUERIES, dtype=jnp.int32)
    starts = jnp.sum((query_ids[None, :] < labels[:, None]).astype(jnp.int32), axis=1)
    window = jnp.minimum(
        starts[:, None] + jnp.arange(QMOST, dtype=jnp.int32)[None, :], token_count - 1
    )
    live_slot = jnp.take(query_ids, window) == labels[:, None]
    return (window, live_slot)


def window_rows(columns, window):
    return jnp.transpose(jnp.take(columns, window, axis=1), (1, 2, 0))


def build_precond(left_window, right_cols, eig_cols, window):
    right_window = window_rows(right_cols, window)
    query_count = left_window.shape[0]
    group_size = math.gcd(query_count, 8)
    left_groups = left_window.reshape(
        (query_count // group_size, group_size) + left_window.shape[1:]
    )
    right_groups = right_window.reshape(
        (query_count // group_size, group_size) + right_window.shape[1:]
    )

    def one_group(operands):
        products = jnp.einsum(
            "qms,qma->qsa", operands[0], operands[1], preferred_element_type=jnp.float32
        )
        return (products / (eig_cols[None] + damping_shift)).astype(jnp.bfloat16)

    precond_groups = lax.map(one_group, (left_groups, right_groups))
    return precond_groups.reshape((query_count,) + precond_groups.shape[2:])


def on_device(
    query_grad,
    query_input,
    query_ids,
    train_grad,
    train_input,
    train_ids,
    output_basis,
    input_basis,
    eigenvalues,
):
    query_left = rotate(output_basis, query_grad)
    query_right = rotate(input_basis, query_input)
    train_left = rotate(output_basis, train_grad)
    train_right = rotate(input_basis, train_input)
    window, live_slot = query_window(query_ids)
    left_taken = window_rows(query_left, window)
    left_window = jnp.where(live_slot[:, :, None], left_taken, jnp.zeros((), jnp.bfloat16))
    right_full, train_full = (
        lax.all_gather(query_right, "mp", axis=0, tiled=True),
        lax.all_gather(train_right, "mp", axis=0, tiled=True),
    )
    precond = build_precond(left_window, right_full, eigenvalues, window)
    inner_sum = jnp.einsum("qsa,at->qst", precond, train_full, preferred_element_type=jnp.float32)
    contrib = jnp.einsum(
        "qst,st->qt", inner_sum, train_left.astype(jnp.float32), precision=lax.Precision.HIGHEST
    )
    onehot = (train_ids[:, None] == jnp.arange(TRAIN, dtype=jnp.int32)[None, :]).astype(jnp.float32)
    shares = jnp.dot(contrib, onehot, precision=lax.Precision.HIGHEST)
    return lax.psum(shares, "mp")


def solution(mesh):
    return jax.shard_map(
        on_device,
        mesh=mesh,
        in_specs=(
            P("grp", None),
            P("grp", None),
            P("grp"),
            P("grp", None),
            P("grp", None),
            P("grp"),
            P(None, "mp"),
            P(None, "mp"),
            P("mp", None),
        ),
        out_specs=P("grp", None),
        check_vma=False,
    )
```

profile of v0, /device:TPU:0, one launch (start us, length us, event | category | flops | bytes accessed | tf_op | source)
XLA Modules:
  0.0 167.1 jit_solution(38802841651659386)
XLA Ops:
  6.5 1.6 copy-done
  8.1 6.4 %convolution_convert_fusion = bf16[512,128]{1,0:T(8,128)(2,1)} fusion(bf16[8192,512]{1,0:T(8,128)(2,1)} %param.16, bf16[128,8192]{1,0:T(8,128)(2,1)S(1)} %copy-done), kind=kOutput, calls=%fused_computation.9 | convolution fusion | flops 1073807360 | bytes 10616832 | tf_op jit(solution)/shard_map/dot_general | solution.py:14
  14.5 0.0 all-gather.2.cloned.1.call-update
  14.6 0.0 copy-done.1
  14.6 0.1 convert_reduce_fusion
  14.7 0.1 compare_select_fusion
  14.8 0.1 reshape.101
  14.9 0.8 gather_fusion
  15.6 0.1 reshape.100
  15.7 0.1 iota_compare_fusion.2
  15.8 0.0 copy-done.3
  15.8 4.9 %convolution_convert_fusion.2 = bf16[512,32]{0,1:T(8,128)(2,1)S(1)} fusion(bf16[32,8192]{1,0:T(8,128)(2,1)S(1)} %copy-done.3, bf16[8192,512]{1,0:T(8,128)(2,1)} %param.16), kind=kOutput, calls=%fused_computation.13 | convolution fusion | flops 268451840 | bytes 8945664 | tf_op jit(solution)/shard_map/dot_general | solution.py:14
  20.7 24.6 %all_gather.6 = bf16[8192,32]{0,1:T(8,128)(2,1)S(1)} all-gather(bf16[512,32]{0,1:T(8,128)(2,1)S(1)} %convolution_convert_fusion.2), channel_id=1, replica_groups=mesh['grp'=2,'mp'=16] {'mp'}, dimensions={0}, use_global_device_ids=true | all-gather | bytes 557056 | tf_op jit(solution)/shard_map/all_gather | solution.py:74
  45.4 2.2 %gather_fusion.2 = bf16[64,8192]{1,0:T(8,128)(2,1)} fusion(bf16[8192,32]{0,1:T(8,128)(2,1)S(1)} %all_gather.6, s32[1024]{0:T(1024)S(1)} %pad_clamp_fusion), kind=kCustom, calls=%fused_computation.2 | custom fusion | bytes 2097408 | tf_op jit(solution)/shard_map/jit(_take)/gather | solution.py:31
  47.6 4.9 %convolution_convert_fusion.3 = bf16[512,32]{0,1:T(8,128)(2,1)S(1)} fusion(bf16[32,8192]{1,0:T(8,128)(2,1)S(1)} %copy-done.4, bf16[8192,512]{1,0:T(8,128)(2,1)} %param.15), kind=kOutput, calls=%fused_computation.14 | convolution fusion | flops 268451840 | bytes 8945664 | tf_op jit(solution)/shard_map/dot_general | solution.py:14
  52.5 0.7 gather_fusion.1
  53.2 11.9 %broadcast_add_fusion = f32[512,8192]{1,0:T(8,128)} fusion(f32[512,8192]{1,0:T(8,128)} %param.17), kind=kLoop, calls=%fused_computation.6 | loop fusion | flops 4194304 | bytes 33554432 | tf_op jit(solution)/shard_map/while/body/eval_jaxpr/add | solution.py:49
  65.1 30.2 %divide_convert_fusion.6 = bf16[8,512,8192]{2,1,0:T(8,128)(2,1)} fusion(f32[512,8192]{1,0:T(8,128)} %broadcast_add_fusion, bf16[64,8192]{1,0:T(8,128)(2,1)S(1)} %copy-done.2, pred[8,8]{1,0:T(8,128)(4,1)S(1)} %get-tuple-element.14, bf16[64,512]{1,0:T(8,128)(2,1)S(1)} %gather_fusion.1, pred[8,8]{1,0:T(8,128)(4,1)S(1)} %get-tuple-element.13), kind=kOutput, calls=%fused_computation.3.clone.clone.clone.clone.1 | convolution fusion | flops 604569600 | bytes 85000320 | tf_op jit(solution)/shard_map/while/body/eval_jaxpr/qms,qma->qsa/dot_general | solution.py:46
  95.3 6.3 %fusion.7 = f32[128,512]{0,1:T(8,128)S(1)} fusion(bf16[8192,512]{1,0:T(8,128)(2,1)} %param.15, bf16[128,8192]{1,0:T(8,128)(2,1)} %param.12), kind=kOutput, calls=%fused_computation.12 | convolution fusion | flops 1073872896 | bytes 10747904 | tf_op jit(solution)/shard_map/dot_general | solution.py:14
  101.7 0.0 copy-start.5
  101.7 0.0 all-gather.2.cloned.1.call-done
  101.7 27.9 %multiply_reduce_fusion = f32[128,8]{0,1:T(8,128)S(1)} fusion(bf16[8192,128]{1,0:T(8,128)(2,1)} %all-gather.2.cloned.1.call-done, f32[128,512]{0,1:T(8,128)S(1)} %fusion.7, bf16[8,512,8192]{2,1,0:T(8,128)(2,1)} %divide_convert_fusion.6), kind=kOutput, calls=%fused_computation.8 | convolution fusion | flops 8590982144 | bytes 69472256 | tf_op jit(solution)/shard_map/qsa,at->qst/dot_general | solution.py:78
  129.7 0.2 fusion.19
  129.8 30.4 %psum.7 = f32[8,16]{1,0:T(8,128)} all-reduce(f32[8,16]{1,0:T(8,128)S(1)} %fusion.19), channel_id=1, replica_groups=mesh['grp'=2,'mp'=16] {'mp'}, use_global_device_ids=true, to_apply=%region_1.2 | all-reduce | flops 128 | bytes 1024 | tf_op jit(solution)/shard_map/psum | solution.py:84
  (10 shorter events, 0.0 us)
Async XLA Ops:
  6.5 1.6 copy-start
  6.5 8.0 %copy-start.1 = (s32[32]{0:T(128)S(1)}, s32[32]{0:T(128)}, u32[]{:S(2)}) copy-start(s32[32]{0:T(128)} %param.11) | copy-start | bytes 388
  6.5 9.3 %copy-start.3 = (bf16[32,8192]{1,0:T(8,128)(2,1)S(1)}, bf16[32,8192]{1,0:T(8,128)(2,1)}, u32[]{:S(2)}) copy-start(bf16[32,8192]{1,0:T(8,128)(2,1)} %param.10) | copy-start | bytes 1572868
  6.5 95.2 %all-gather.2.cloned.1.call-start = ((), (), s32[]{:S(2)}) async-start(), calls=%async_computation | async-start | bytes 2228224 | tf_op jit(solution)/shard_map/all_gather | solution.py:75
  45.4 2.2 %copy-start.4 = (bf16[32,8192]{1,0:T(8,128)(2,1)S(1)}, bf16[32,8192]{1,0:T(8,128)(2,1)}, u32[]{:S(2)}) copy-start(bf16[32,8192]{1,0:T(8,128)(2,1)} %param.9) | copy-start | bytes 1572868
  53.2 11.9 %copy-start.2 = (bf16[64,8192]{1,0:T(8,128)(2,1)S(1)}, bf16[64,8192]{1,0:T(8,128)(2,1)}, u32[]{:S(2)}) copy-start(bf16[64,8192]{1,0:T(8,128)(2,1)} %gather_fusion.2) | copy-start | bytes 3145732
  101.7 28.0 %copy-start.5 = (s32[128]{0:T(128)S(1)}, s32[128]{0:T(128)}, u32[]{:S(2)}) copy-start(s32[128]{0:T(128)} %param.14) | copy-start | bytes 1540
Sparse Core Ops, SparseCore 0:
  14.7 44.4 all-gather.1
where the time goes:
time: 167 us
  matrix products  81 us (49%)
  blocking collectives  55.1 us (33%)
  between operations  13.5 us (8%)
  other arithmetic  12.1 us (7%)
  local copies, waits for them, and re-layouts  5.45 us (3%)
    psum x1, blocking collectives, on_device(): return lax.psum(shares, 'mp')  30.4 us
    dot_general x1, matrix products, one_group(): jnp.einsum('qms,qma->qsa', operands[0], operands[1], preferred_element_ty...  30.2 us
    dot_general x1, matrix products, on_device(): jnp.einsum('qsa,at->qst', precond, train_full, preferred_element_type=jnp...  27.9 us
    all_gather x1, blocking collectives, on_device(): lax.all_gather(query_right, 'mp', axis=0, tiled=True)  24.6 us
    dot_general x4, matrix products, rotate(): lax.dot_general(basis, factors, (((0,), (1,)), ((), ())), preferred_eleme...  22.6 us
    add x1, other arithmetic, one_group(): return (products / (eig_cols[None] + damping_shift)).astype(jnp.bfloat16)  11.9 us
  transfers between devices with their start and end apart: 1, of which 0 were waited for; matrix products, arithmetic and copies ran while one was open for 37% of the time, Pallas kernels for 0%

commit v1 on v0

--- a/solution.py
+++ b/solution.py
@@ -8,6 +8,18 @@
 QMOST = 8
 TRAIN = 16
 damping_shift = 0.25
+
+
+def collect(x, axis, dim):
+    ways, here, step = (lax.axis_size(axis), lax.axis_index(axis), x.shape[dim])
+    line, have = (x, 1)
+    while have < ways:
+        line = jnp.concatenate(
+            [line, lax.ppermute(line, axis, [(d, (d - have) % ways) for d in range(ways)])],
+            axis=dim,
+        )
+        have = 2 * have
+    return jnp.roll(line, here * step, axis=dim)
 
 
 def rotate(basis, factors):
@@ -71,7 +83,7 @@
     left_taken = window_rows(query_left, window)
     left_window = jnp.where(live_slot[:, :, None], left_taken, jnp.zeros((), jnp.bfloat16))
     right_full, train_full = (
-        lax.all_gather(query_right, "mp", axis=0, tiled=True),
+        collect(query_right, "mp", 0),
         lax.all_gather(train_right, "mp", axis=0, tiled=True),
     )
     precond = build_precond(left_window, right_full, eigenvalues, window)

time: 167 us -> 178 us (1.066)
  blocking collectives: 55.1 us -> 33.8 us
  waiting for transfers between devices: 0.04 us -> 20.9 us
  starting transfers between devices: 0.01 us -> 7.07 us
  local copies, waits for them, and re-layouts: 5.45 us -> 10.8 us
    all_gather x1 -> x0, blocking collectives: 24.6 us -> none  [on_device(): lax.all_gather(query_right, 'mp', axis=0, tiled=True)]
    ppermute x0 -> x4, waiting for transfers between devices: none -> 20.9 us  [collect(): lax.ppermute(line, axis, [(d, (d - have) % ways) for d in range(ways)])]
    ppermute x0 -> x4, starting transfers between devices: none -> 7.07 us  [collect(): lax.ppermute(line, axis, [(d, (d - have) % ways) for d in range(ways)])]
    unnamed x12 -> x22, local copies, waits for them, and re-layouts: 1.61 us -> 5.19 us
    psum x1, blocking collectives: 30.4 us -> 33.8 us  [on_device(): return lax.psum(shares, 'mp')]
    dot_general x4, matrix products: 22.6 us -> 20.3 us  [rotate(): lax.dot_general(basis, factors, (((0,), (1,)), ((), ())), preferred_eleme...]
  transfers between devices with their start and end apart: 1 -> 5, of which waited for: 0 -> 3; matrix products, arithmetic and copies ran while one was open for 37% -> 39% of each run, Pallas kernels for 0% -> 0%
where the time goes in v1:
time: 178 us
  matrix products  79.6 us (45%)
  blocking collectives  33.8 us (19%)
  waiting for transfers between devices  20.9 us (12%)
  between operations  13.5 us (8%)
  other arithmetic  12 us (7%)
  local copies, waits for them, and re-layouts  10.8 us (6%)
  starting transfers between devices  7.07 us (4%)
    psum x1, blocking collectives, on_device(): return lax.psum(shares, 'mp')  33.8 us
    dot_general x1, matrix products, one_group(): jnp.einsum('qms,qma->qsa', operands[0], operands[1], preferred_element_ty...  31.1 us
    dot_general x1, matrix products, on_device(): jnp.einsum('qsa,at->qst', precond, train_full, preferred_element_type=jnp...  27.9 us
    ppermute x4, waiting for transfers between devices, collect(): lax.ppermute(line, axis, [(d, (d - have) % ways) for d in range(ways)])  20.9 us
    dot_general x4, matrix products, rotate(): lax.dot_general(basis, factors, (((0,), (1,)), ((), ())), preferred_eleme...  20.3 us
    add x1, other arithmetic, one_group(): return (products / (eig_cols[None] + damping_shift)).astype(jnp.bfloat16)  11.6 us
    ppermute x4, starting transfers between devices, collect(): lax.ppermute(line, axis, [(d, (d - have) % ways) for d in range(ways)])  7.07 us
    unnamed x22, local copies, waits for them, and re-layouts  5.19 us
  transfers between devices with their start and end apart: 5, of which 3 were waited for; matrix products, arithmetic and copies ran while one was open for 39% of the time, Pallas kernels for 0%

profile of v1, /device:TPU:0, one launch (start us, length us, event | category | flops | bytes accessed | tf_op | source)
XLA Modules:
  0.0 177.6 jit_solution(11696945178573772565)
XLA Ops:
  6.5 5.8 %constant_dynamic-update-slice_fusion.9 = (bf16[16384,32]{0,1:T(8,128)(2,1)}, bf16[512,32]{0,1:T(8,128)(2,1)S(1)}) fusion(bf16[32,8192]{1,0:T(8,128)(2,1)} %param.10, bf16[8192,512]{1,0:T(8,128)(2,1)} %param.16), kind=kOutput, calls=%fused_computation.39 | convolution fusion | flops 268451840 | bytes 8978432 | tf_op jit(solution)/shard_map/dot_general | solution.py:26
  12.4 5.4 %collective-permute-start = (bf16[512,32]{0,1:T(8,128)(2,1)S(1)}, bf16[512,32]{0,1:T(8,128)(2,1)S(1)}, u32[]{:S(2)}, u32[]{:S(2)}) collective-permute-start(bf16[512,32]{0,1:T(8,128)(2,1)S(1)} %get-tuple-element.22), channel_id=1, source_target_pairs={{0,15},{1,0},{2,1},{3,2},{4,3},{5,4},{6,5},{7,6},{8,7},{9,8},{10,9... | collective-permute-start | bytes 98312 | tf_op jit(solution)/shard_map/ppermute | solution.py:18
  17.8 3.0 %convolution_convert_fusion = bf16[512,128]{1,0:T(8,128)(2,1)} fusion(bf16[8192,512]{1,0:T(8,128)(2,1)S(1)} %copy-done.2, bf16[128,8192]{1,0:T(8,128)(2,1)S(1)} %copy-done), kind=kOutput, calls=%fused_computation.9 | convolution fusion | flops 1073807360 | bytes 10616832 | tf_op jit(solution)/shard_map/dot_general | solution.py:26
  21.0 11.6 %broadcast_add_fusion = f32[512,8192]{1,0:T(8,128)} fusion(f32[512,8192]{1,0:T(8,128)} %param.17), kind=kLoop, calls=%fused_computation.6 | loop fusion | flops 4194304 | bytes 33554432 | tf_op jit(solution)/shard_map/while/body/eval_jaxpr/add | solution.py:61
  32.6 5.0 %convolution_convert_fusion.3 = bf16[512,32]{0,1:T(8,128)(2,1)S(1)} fusion(bf16[32,8192]{1,0:T(8,128)(2,1)S(1)} %copy-done.3, bf16[8192,512]{1,0:T(8,128)(2,1)} %param.15), kind=kOutput, calls=%fused_computation.14 | convolution fusion | flops 268451840 | bytes 8945664 | tf_op jit(solution)/shard_map/dot_general | solution.py:26
  37.7 6.4 %fusion.7 = f32[128,512]{0,1:T(8,128)} fusion(bf16[8192,512]{1,0:T(8,128)(2,1)} %param.15, bf16[128,8192]{1,0:T(8,128)(2,1)S(1)} %copy-done.4), kind=kOutput, calls=%fused_computation.12 | convolution fusion | flops 1073872896 | bytes 10747904 | tf_op jit(solution)/shard_map/dot_general | solution.py:26
  44.3 1.3 collective-permute-start.1
  45.6 0.8 gather_fusion
  46.5 3.5 %collective-permute-done.1 = bf16[1024,32]{0,1:T(8,128)(2,1)S(1)} collective-permute-done((bf16[1024,32]{0,1:T(8,128)(2,1)S(1)}, bf16[1024,32]{0,1:T(8,128)(2,1)S(1)}, u32[]{:S(2)}, u32[]{:S(2)}) %collective-permute-start.1) | collective-permute-done | bytes 65568 | tf_op jit(solution)/shard_map/ppermute | solution.py:18
  50.3 0.7 gather_fusion.1
  51.6 5.6 %collective-permute-done.2 = bf16[2048,32]{0,1:T(8,128)(2,1)S(1)} collective-permute-done((bf16[2048,32]{0,1:T(8,128)(2,1)S(1)}, bf16[2048,32]{0,1:T(8,128)(2,1)S(1)}, u32[]{:S(2)}, u32[]{:S(2)}) %collective-permute-start.2) | collective-permute-done | bytes 131104 | tf_op jit(solution)/shard_map/ppermute | solution.py:18
  57.3 0.6 constant_dynamic-update-slice_fusion.7
  58.0 0.7 constant_dynamic-update-slice_fusion.6
  58.6 11.8 %collective-permute-done.3 = bf16[4096,32]{0,1:T(8,128)(2,1)S(1)} collective-permute-done((bf16[4096,32]{0,1:T(8,128)(2,1)S(1)}, bf16[4096,32]{0,1:T(8,128)(2,1)S(1)}, u32[]{:S(2)}, u32[]{:S(2)}) %collective-permute-start.3) | collective-permute-done | bytes 262176 | tf_op jit(solution)/shard_map/ppermute | solution.py:18
  70.4 0.7 constant_dynamic-update-slice_fusion.5
  71.8 0.6 constant_dynamic-update-slice_fusion.3
  72.4 0.6 constant_dynamic-update-slice_fusion.2
  73.0 0.7 constant_dynamic-update-slice_fusion.1
  73.7 0.7 constant_dynamic-update-slice_fusion
  74.4 1.1 constant_dynamic-slice_fusion
  75.5 2.2 %gather_fusion.2 = bf16[64,8192]{1,0:T(8,128)(2,1)} fusion(bf16[8192,32]{0,1:T(8,128)(2,1)S(1)} %constant_dynamic-slice_fusion, s32[1024]{0:T(1024)S(1)} %pad_clamp_fusion), kind=kCustom, calls=%fused_computation.2 | custom fusion | bytes 2097408 | tf_op jit(solution)/shard_map/jit(_take)/gather | solution.py:43
  77.7 31.1 %divide_convert_fusion.6 = bf16[8,512,8192]{2,1,0:T(8,128)(2,1)} fusion(f32[512,8192]{1,0:T(8,128)} %broadcast_add_fusion, bf16[64,8192]{1,0:T(8,128)(2,1)} %gather_fusion.2, pred[8,8]{1,0:T(8,128)(4,1)S(1)} %get-tuple-element.14, bf16[64,512]{1,0:T(8,128)(2,1)S(1)} %gather_fusion.1, pred[8,8]{1,0:T(8,128)(4,1)S(1)} %get-tuple-element.13), kind=kOutput, calls=%fused_computation.3.clone.clone.clone.clone.1 | convolution fusion | flops 604569600 | bytes 85000320 | tf_op jit(solution)/shard_map/while/body/eval_jaxpr/qms,qma->qsa/dot_general | solution.py:58
  108.9 27.9 %multiply_reduce_fusion = f32[128,8]{0,1:T(8,128)S(1)} fusion(bf16[8192,128]{1,0:T(8,128)(2,1)} %all-gather.2.cloned.1.call-done, f32[128,512]{0,1:T(8,128)S(1)} %copy-done.6, bf16[8,512,8192]{2,1,0:T(8,128)(2,1)} %divide_convert_fusion.6), kind=kOutput, calls=%fused_computation.8 | convolution fusion | flops 8590982144 | bytes 69472256 | tf_op jit(solution)/shard_map/qsa,at->qst/dot_general | solution.py:90
  137.0 33.8 %psum.7 = f32[8,16]{1,0:T(8,128)} all-reduce(f32[8,16]{1,0:T(8,128)S(1)} %fusion.19), channel_id=1, replica_groups=mesh['grp'=2,'mp'=16] {'mp'}, use_global_device_ids=true, to_apply=%region_1.2 | all-reduce | flops 128 | bytes 1024 | tf_op jit(solution)/shard_map/psum | solution.py:96
  (32 shorter events, 2.2 us)
Async XLA Ops:
  6.5 11.3 %copy-start = (bf16[128,8192]{1,0:T(8,128)(2,1)S(1)}, bf16[128,8192]{1,0:T(8,128)(2,1)}, u32[]{:S(2)}) copy-start(bf16[128,8192]{1,0:T(8,128)(2,1)} %param.13) | copy-start | bytes 6291460
  6.5 102.3 %all-gather.2.cloned.1.call-start = ((), (), s32[]{:S(2)}) async-start(), calls=%async_computation | async-start | bytes 2228224 | tf_op jit(solution)/shard_map/all_gather | solution.py:87
  6.5 11.3 %copy-start.2 = (bf16[8192,512]{1,0:T(8,128)(2,1)S(1)}, bf16[8192,512]{1,0:T(8,128)(2,1)}, u32[]{:S(2)}) copy-start(bf16[8192,512]{1,0:T(8,128)(2,1)} %param.16) | copy-start | bytes 25165828
  12.4 8.5 %copy-start.1 = (s32[32]{0:T(128)S(1)}, s32[32]{0:T(128)}, u32[]{:S(2)}) copy-start(s32[32]{0:T(128)} %param.11) | copy-start | bytes 388
  12.4 31.9 %collective-permute-start = (bf16[512,32]{0,1:T(8,128)(2,1)S(1)}, bf16[512,32]{0,1:T(8,128)(2,1)S(1)}, u32[]{:S(2)}, u32[]{:S(2)}) collective-permute-start(bf16[512,32]{0,1:T(8,128)(2,1)S(1)} %get-tuple-element.22), channel_id=1, source_target_pairs={{0,15},{1,0},{2,1},{3,2},{4,3},{5,4},{6,5},{7,6},{8,7},{9,8},{10,9... | collective-permute-start | bytes 98312 | tf_op jit(solution)/shard_map/ppermute | solution.py:18
  21.0 11.7 %copy-start.3 = (bf16[32,8192]{1,0:T(8,128)(2,1)S(1)}, bf16[32,8192]{1,0:T(8,128)(2,1)}, u32[]{:S(2)}) copy-start(bf16[32,8192]{1,0:T(8,128)(2,1)} %param.9) | copy-start | bytes 1572868
  32.6 5.1 %copy-start.4 = (bf16[128,8192]{1,0:T(8,128)(2,1)S(1)}, bf16[128,8192]{1,0:T(8,128)(2,1)}, u32[]{:S(2)}) copy-start(bf16[128,8192]{1,0:T(8,128)(2,1)} %param.12) | copy-start | bytes 6291460
  44.3 5.7 %collective-permute-start.1 = (bf16[1024,32]{0,1:T(8,128)(2,1)S(1)}, bf16[1024,32]{0,1:T(8,128)(2,1)S(1)}, u32[]{:S(2)}, u32[]{:S(2)}) collective-permute-start(bf16[1024,32]{0,1:T(8,128)(2,1)S(1)} %pad_maximum_fusion.2), channel_id=1, source_target_pairs={{0,14},{1,15},{2,0},{3,1},{4,2},{5,3},{6,4},{7,5},{8,6},{9,7},{10,... | collective-permute-start | bytes 196616 | tf_op jit(solution)/shard_map/ppermute | solution.py:18
  50.0 7.3 %collective-permute-start.2 = (bf16[2048,32]{0,1:T(8,128)(2,1)S(1)}, bf16[2048,32]{0,1:T(8,128)(2,1)S(1)}, u32[]{:S(2)}, u32[]{:S(2)}) collective-permute-start(bf16[2048,32]{0,1:T(8,128)(2,1)S(1)} %pad_maximum_fusion.1), channel_id=1, source_target_pairs={{0,12},{1,13},{2,14},{3,15},{4,0},{5,1},{6,2},{7,3},{8,4},{9,5},{1... | collective-permute-start | bytes 393224 | tf_op jit(solution)/shard_map/ppermute | solution.py:18
  57.3 13.2 %collective-permute-start.3 = (bf16[4096,32]{0,1:T(8,128)(2,1)S(1)}, bf16[4096,32]{0,1:T(8,128)(2,1)S(1)}, u32[]{:S(2)}, u32[]{:S(2)}) collective-permute-start(bf16[4096,32]{0,1:T(8,128)(2,1)S(1)} %pad_maximum_fusion), channel_id=1, source_target_pairs={{0,8},{1,9},{2,10},{3,11},{4,12},{5,13},{6,14},{7,15},{8,0},{9,1},... | collective-permute-start | bytes 786440 | tf_op jit(solution)/shard_map/ppermute | solution.py:18
  77.7 31.2 %copy-start.6 = (f32[128,512]{0,1:T(8,128)S(1)}, f32[128,512]{0,1:T(8,128)}, u32[]{:S(2)}) copy-start(f32[128,512]{0,1:T(8,128)} %fusion.7) | copy-start | bytes 786436
  108.9 27.9 %copy-start.5 = (s32[128]{0:T(128)S(1)}, s32[128]{0:T(128)}, u32[]{:S(2)}) copy-start(s32[128]{0:T(128)} %param.14) | copy-start | bytes 1540
Sparse Core Ops, SparseCore 0:
  21.0 41.8 all-gather.1
